TPU v7x, 32 devices: a whole 2x2x4 slice. The times are simulated.
32 devices in a mesh: dp: 4 (over y, x), fsdp: 8 (over z, core).
Axes of the slice: x: 2, y: 2, z: 4, core: 2. Of those that a mesh axis runs over, the one named last changes fastest.
Arguments:
- images: bfloat16 [128, 282, 768], P(('dp', 'fsdp')), may hold values from -18 to 18
- grid_sizes: int32 [128, 2], P(('dp', 'fsdp')), may hold values from 8 to 24, as said below
- keep_flags: int32 [128, 2], P(('dp', 'fsdp')), may hold values 0 or 1
- attn_gain: bfloat16 [768], P('fsdp'), may hold values from 0.25 to 1.75
- attn_shift: bfloat16 [768], P('fsdp'), may hold values from -4 to 4
- attend_weight: bfloat16 [768, 2304], P(None, 'fsdp'), may hold values from -0.3125 to 0.3125
- query_bias: bfloat16 [768], P('fsdp'), may hold values from -6 to 6
- value_bias: bfloat16 [768], P('fsdp'), may hold values from -6 to 6
- output_weight: bfloat16 [768, 768], P('fsdp'), may hold values from -1.25 to 1.25
- output_bias: bfloat16 [768], P('fsdp'), may hold values from -4 to 4
- mlp_gain: bfloat16 [768], P('fsdp'), may hold values from 0.25 to 1.75
- mlp_shift: bfloat16 [768], P('fsdp'), may hold values from -4 to 4
- up_weight: bfloat16 [768, 3072], P(None, 'fsdp'), may hold values from -0.21875 to 0.21875
- up_bias: bfloat16 [3072], P('fsdp'), may hold values from -6 to 6
- down_weight: bfloat16 [3072, 768], P('fsdp'), may hold values from -0.15625 to 0.15625
- down_bias: bfloat16 [768], P('fsdp'), may hold values from -4 to 4
- cotangent: bfloat16 [128, 282, 768], P(('dp', 'fsdp')), may hold values from -6 to 6
Outputs:
- output: bfloat16 [128, 282, 768], P(('dp', 'fsdp'))
- grad_images: float32 [128, 282, 768], P(('dp', 'fsdp'))
- grad_attn_gain: float32 [768], P('fsdp')
- grad_attn_shift: float32 [768], P('fsdp')
- grad_attend_weight: float32 [768, 2304], P(None, 'fsdp')
- grad_query_bias: float32 [768], P('fsdp')
- grad_value_bias: float32 [768], P('fsdp')
- grad_output_weight: float32 [768, 768], P('fsdp')
- grad_output_bias: float32 [768], P('fsdp')
- grad_mlp_gain: float32 [768], P('fsdp')
- grad_mlp_shift: float32 [768], P('fsdp')
- grad_up_weight: float32 [768, 3072], P(None, 'fsdp')
- grad_up_bias: float32 [3072], P('fsdp')
- grad_down_weight: float32 [3072, 768], P('fsdp')
- grad_down_bias: float32 [768], P('fsdp')
- root_means: float32 [3], replicated
Inputs may be any that keep to these rules, and one draw needn't show every extreme that they name: `grid_sizes`: each image has rows from 8 to 20 and cols at most min(24, 280 // rows) and at least min(24, 280 // rows) - 2; its first rows * cols + 2 token slots are valid, at most 282. Image 0 has 20 x 14, filling all 282 slots; image 1 has 8 rows.
All inputs are finite; a program needn't handle non-finite values. No bound on the sum of `keep_flags` on one device may be relied on, other than what follows from the above.
Results may differ from a plain program's by a relative error of at most 0.015.
The roundings to bfloat16 on the way count: a program that leaves them out, or rounds other values in their place, can miss the bound.
Values may be sent and summed in bfloat16 or wider, within the bound.
No kernel may reach another device: no remote copies, remote signals or barrier semaphores. Data moves between devices by JAX's collectives and lax.ppermute only.
A program may use at most 192 MiB of HBM per device.

v0:
```python
import math

import jax
import jax.numpy as jnp
from jax import lax
from jax.sharding import PartitionSpec as P

HEADS = 12
HEAD_DIM = 64


EPS = 1e-06
KEEP_PROB = 0.9
MASKED = -1e30
INV_ROOT_TWO = 0.7071067811865476
INV_ROOT_TWO_PI = 0.3989422804014327


def product(formula, left, right):
    return jnp.einsum(formula, left, right, preferred_element_type=jnp.float32)


def normalize(values):
    center = values - jnp.mean(values, -1, keepdims=True)
    rstd_row = lax.rsqrt(jnp.mean(center * center, -1, keepdims=True) + EPS)
    return (center * rstd_row, rstd_row)


def norm_back(grad_normed, normed, rstd_row, gain_full):
    grad_hat = grad_normed * gain_full
    return rstd_row * (
        grad_hat
        - jnp.mean(grad_hat, -1, keepdims=True)
        - normed * jnp.mean(grad_hat * normed, -1, keepdims=True)
    )


def scores_of(query, keys_in, valid_keys):
    scores = product("bqhe,bkhe->bhqk", query, keys_in) * (1.0 / math.sqrt(HEAD_DIM))
    return jnp.where(valid_keys[:, None, None, :] > 0, scores, MASKED)


def attend_block(inputs):
    query, keys_in, values_in, valid_keys = inputs
    scores = scores_of(query, keys_in, valid_keys)
    top_score = jnp.max(scores, -1, keepdims=True)
    unnormed = jnp.exp(scores - top_score)
    total = jnp.sum(unnormed, -1, keepdims=True)
    probability = unnormed / total
    mixed = product("bhqk,bkhe->bqhe", probability.astype(jnp.bfloat16), values_in)
    log_total = top_score[..., 0] + jnp.log(total[..., 0])
    return (mixed.astype(jnp.bfloat16), log_total)


def attend_back(inputs):
    query, keys_in, values_in, valid_keys, log_total, grad_mixed = inputs
    scores = scores_of(query, keys_in, valid_keys)
    probability = jnp.exp(scores - log_total[..., None])
    grad_values = product("bhqk,bqhe->bkhe", probability.astype(jnp.bfloat16), grad_mixed)
    grad_prob = product("bqhe,bkhe->bhqk", grad_mixed, values_in)
    inner = jnp.sum(probability * grad_prob, -1, keepdims=True)
    grad_scores = (probability * (grad_prob - inner)).astype(jnp.bfloat16)
    factor = 1.0 / math.sqrt(HEAD_DIM)
    grad_query = product("bhqk,bkhe->bqhe", grad_scores, keys_in) * factor
    grad_keys = product("bhqk,bqhe->bkhe", grad_scores, query) * factor
    return (
        grad_query.astype(jnp.bfloat16),
        grad_keys.astype(jnp.bfloat16),
        grad_values.astype(jnp.bfloat16),
    )


def shards(
    images,
    grid_sizes,
    keep_flags,
    attn_gain,
    attn_shift,
    attend_weight,
    query_bias,
    value_bias,
    output_weight,
    output_bias,
    mlp_gain,
    mlp_shift,
    up_weight,
    up_bias,
    down_weight,
    down_bias,
    cotangent,
):
    image_count, seq_len, feature_dim = images.shape
    counts = grid_sizes[:, 0] * grid_sizes[:, 1] + 2
    valid = (jnp.arange(seq_len)[None, :] < counts[:, None]).astype(jnp.float32)
    row_mask = valid[:, :, None]
    depth_scale = keep_flags.astype(jnp.float32) / KEEP_PROB
    scale_attn = depth_scale[:, 0, None, None]
    scale_mlp = depth_scale[:, 1, None, None]
    block_size = min(2, image_count)

    def blocks(array):
        return array.reshape((image_count // block_size, block_size) + array.shape[1:])

    gain_first, shift_first, attend_whole, bias_query, bias_value, output_whole, bias_output = (
        lax.all_gather(attn_gain, "fsdp", axis=0, tiled=True),
        lax.all_gather(attn_shift, "fsdp", axis=0, tiled=True),
        lax.all_gather(attend_weight, "fsdp", axis=1, tiled=True),
        lax.all_gather(query_bias, "fsdp", axis=0, tiled=True),
        lax.all_gather(value_bias, "fsdp", axis=0, tiled=True),
        lax.all_gather(output_weight, "fsdp", axis=0, tiled=True),
        lax.all_gather(output_bias, "fsdp", axis=0, tiled=True),
    )
    inputs = images.astype(jnp.float32)
    normed_first, rstd_first = normalize(inputs)
    gain_one = gain_first.astype(jnp.float32)
    ln_first = (normed_first * gain_one + shift_first.astype(jnp.float32)).astype(jnp.bfloat16)
    bias_joint = jnp.concatenate([bias_query, jnp.zeros_like(bias_query), bias_value]).astype(
        jnp.float32
    )
    joint = (product("bld,de->ble", ln_first, attend_whole) + bias_joint).astype(jnp.bfloat16)
    joint = joint.reshape(image_count, seq_len, 3, HEADS, HEAD_DIM)
    query = blocks(joint[:, :, 0])
    keys_in = blocks(joint[:, :, 1])
    values_in = blocks(joint[:, :, 2])
    valid_blocks = blocks(valid)
    mixed_blocks, log_total = lax.map(attend_block, (query, keys_in, values_in, valid_blocks))
    mixed = mixed_blocks.reshape(image_count, seq_len, feature_dim)
    attn_out = product("bld,de->ble", mixed, output_whole) + bias_output.astype(jnp.float32)
    middle = inputs + scale_attn * attn_out
    gain_second, shift_second, up_whole, bias_up, down_whole, bias_down = (
        lax.all_gather(mlp_gain, "fsdp", axis=0, tiled=True),
        lax.all_gather(mlp_shift, "fsdp", axis=0, tiled=True),
        lax.all_gather(up_weight, "fsdp", axis=1, tiled=True),
        lax.all_gather(up_bias, "fsdp", axis=0, tiled=True),
        lax.all_gather(down_weight, "fsdp", axis=0, tiled=True),
        lax.all_gather(down_bias, "fsdp", axis=0, tiled=True),
    )
    normed_second, rstd_second = normalize(middle)
    gain_two = gain_second.astype(jnp.float32)
    ln_second = (normed_second * gain_two + shift_second.astype(jnp.float32)).astype(jnp.bfloat16)
    hidden_pre = product("bld,df->blf", ln_second, up_whole) + bias_up.astype(jnp.float32)
    activated = jax.nn.gelu(hidden_pre, approximate=False).astype(jnp.bfloat16)
    mlp_out = product("blf,fd->bld", activated, down_whole) + bias_down.astype(jnp.float32)
    result = row_mask * (middle + scale_mlp * mlp_out)
    sums = lax.psum(
        (
            jnp.sum(row_mask * middle * middle),
            jnp.sum(row_mask * attn_out * attn_out),
            jnp.sum(row_mask * mlp_out * mlp_out),
            jnp.sum(valid),
        ),
        ("dp", "fsdp"),
    )
    root_means = jnp.sqrt(jnp.stack([sums[0], sums[1], sums[2]]) / (sums[3] * feature_dim))
    grad_out = cotangent.astype(jnp.float32) * row_mask
    grad_mlp = (scale_mlp * grad_out).astype(jnp.bfloat16)
    grad_down_bias = jnp.sum(grad_mlp.astype(jnp.float32), axis=(0, 1))
    grad_act = product("bld,fd->blf", grad_mlp, down_whole)
    cumulative = 0.5 * (1.0 + lax.erf(hidden_pre * INV_ROOT_TWO))
    density = jnp.exp(-0.5 * hidden_pre * hidden_pre) * INV_ROOT_TWO_PI
    grad_hidden = (grad_act * (cumulative + hidden_pre * density)).astype(jnp.bfloat16)
    grad_up_bias = jnp.sum(grad_hidden.astype(jnp.float32), axis=(0, 1))
    grad_ln_second = product("blf,df->bld", grad_hidden, up_whole)
    grad_gain_second = jnp.sum(grad_ln_second * normed_second, axis=(0, 1))
    grad_shift_second = jnp.sum(grad_ln_second, axis=(0, 1))
    grad_middle = grad_out + norm_back(grad_ln_second, normed_second, rstd_second, gain_two)
    grad_down_weight = product("blf,bld->fd", activated, grad_mlp)
    grad_up_weight = product("bld,blf->df", ln_second, grad_hidden)
    mlp_shares = (
        lax.psum_scatter(grad_gain_second, "fsdp", scatter_dimension=0, tiled=True),
        lax.psum_scatter(grad_shift_second, "fsdp", scatter_dimension=0, tiled=True),
        lax.psum_scatter(grad_up_weight, "fsdp", scatter_dimension=1, tiled=True),
        lax.psum_scatter(grad_up_bias, "fsdp", scatter_dimension=0, tiled=True),
        lax.psum_scatter(grad_down_weight, "fsdp", scatter_dimension=0, tiled=True),
        lax.psum_scatter(grad_down_bias, "fsdp", scatter_dimension=0, tiled=True),
    )
    grad_attn = (scale_attn * grad_middle).astype(jnp.bfloat16)
    grad_output_bias = jnp.sum(grad_attn.astype(jnp.float32), axis=(0, 1))
    grad_mixed = product("ble,de->bld", grad_attn, output_whole).astype(jnp.bfloat16)
    grad_mixed = blocks(grad_mixed.reshape(image_count, seq_len, HEADS, HEAD_DIM))
    grad_query, grad_keys, grad_values = lax.map(
        attend_back, (query, keys_in, values_in, valid_blocks, log_total, grad_mixed)
    )
    grad_query = grad_query.reshape(image_count, seq_len, feature_dim)
    grad_keys = grad_keys.reshape(image_count, seq_len, feature_dim)
    grad_values = grad_values.reshape(image_count, seq_len, feature_dim)
    grad_joint = jnp.concatenate([grad_query, grad_keys, grad_values], -1)
    grad_query_bias = jnp.sum(grad_query.astype(jnp.float32), axis=(0, 1))
    grad_value_bias = jnp.sum(grad_values.astype(jnp.float32), axis=(0, 1))
    grad_ln_first = product("ble,de->bld", grad_joint, attend_whole)
    grad_gain_first = jnp.sum(grad_ln_first * normed_first, axis=(0, 1))
    grad_shift_first = jnp.sum(grad_ln_first, axis=(0, 1))
    grad_images = grad_middle + norm_back(grad_ln_first, normed_first, rstd_first, gain_one)
    grad_output_weight = product("bld,ble->de", mixed, grad_attn)
    grad_attend_weight = product("bld,ble->de", ln_first, grad_joint)
    attn_shares = (
        lax.psum_scatter(grad_gain_first, "fsdp", scatter_dimension=0, tiled=True),
        lax.psum_scatter(grad_shift_first, "fsdp", scatter_dimension=0, tiled=True),
        lax.psum_scatter(grad_attend_weight, "fsdp", scatter_dimension=1, tiled=True),
        lax.psum_scatter(grad_query_bias, "fsdp", scatter_dimension=0, tiled=True),
        lax.psum_scatter(grad_value_bias, "fsdp", scatter_dimension=0, tiled=True),
        lax.psum_scatter(grad_output_weight, "fsdp", scatter_dimension=0, tiled=True),
        lax.psum_scatter(grad_output_bias, "fsdp", scatter_dimension=0, tiled=True),
    )
    totals = (
        lax.psum(attn_shares[0].astype(jnp.bfloat16), "dp").astype(jnp.float32),
        lax.psum(attn_shares[1].astype(jnp.bfloat16), "dp").astype(jnp.float32),
        lax.psum(attn_shares[2].astype(jnp.bfloat16), "dp").astype(jnp.float32),
        lax.psum(attn_shares[3].astype(jnp.bfloat16), "dp").astype(jnp.float32),
        lax.psum(attn_shares[4].astype(jnp.bfloat16), "dp").astype(jnp.float32),
        lax.psum(attn_shares[5].astype(jnp.bfloat16), "dp").astype(jnp.float32),
        lax.psum(attn_shares[6].astype(jnp.bfloat16), "dp").astype(jnp.float32),
        lax.psum(mlp_shares[0].astype(jnp.bfloat16), "dp").astype(jnp.float32),
        lax.psum(mlp_shares[1].astype(jnp.bfloat16), "dp").astype(jnp.float32),
        lax.psum(mlp_shares[2].astype(jnp.bfloat16), "dp").astype(jnp.float32),
        lax.psum(mlp_shares[3].astype(jnp.bfloat16), "dp").astype(jnp.float32),
        lax.psum(mlp_shares[4].astype(jnp.bfloat16), "dp").astype(jnp.float32),
        lax.psum(mlp_shares[5].astype(jnp.bfloat16), "dp").astype(jnp.float32),
    )
    return (
        result.astype(jnp.bfloat16),
        grad_images,
        totals[0],
        totals[1],
        totals[2],
        totals[3],
        totals[4],
        totals[5],
        totals[6],
        totals[7],
        totals[8],
        totals[9],
        totals[10],
        totals[11],
        totals[12],
        root_means,
    )


def solution(mesh):
    placed = (
        P(("dp", "fsdp"), None, None),
        P(("dp", "fsdp"), None),
        P(("dp", "fsdp"), None),
        P("fsdp"),
        P("fsdp"),
        P(None, "fsdp"),
        P("fsdp"),
        P("fsdp"),
        P("fsdp", None),
        P("fsdp"),
        P("fsdp"),
        P("fsdp"),
        P(None, "fsdp"),
        P("fsdp"),
        P("fsdp", None),
        P("fsdp"),
        P(("dp", "fsdp"), None, None),
    )
    return jax.shard_map(
        shards,
        mesh=mesh,
        in_specs=placed,
        out_specs=(
            P(("dp", "fsdp"), None, None),
            P(("dp", "fsdp"), None, None),
            P("fsdp"),
            P("fsdp"),
            P(None, "fsdp"),
            P("fsdp"),
            P("fsdp"),
            P("fsdp", None),
            P("fsdp"),
            P("fsdp"),
            P("fsdp"),
            P(None, "fsdp"),
            P("fsdp"),
            P("fsdp", None),
            P("fsdp"),
            P(),
        ),
        check_vma=False,
    )
```

profile of v0, /device:TPU:0, one launch (start us, length us, event | category | flops | bytes accessed | tf_op | source)
XLA Modules:
  0.0 699.8 jit_solution(17826668433202281192)
XLA Ops:
  18.8 31.6 %all-reduce.19 = (bf16[768]{0:T(1024)(128)(2,1)S(1)}, bf16[768]{0:T(1024)(128)(2,1)S(1)}, bf16[768]{0:T(1024)(128)(2,1)S(1)}, bf16[768]{0:T(1024)(128)(2,1)S(1)}...) all-reduce(bf16[768]{0:T(1024)(128)(2,1)S(1)} %dynamic-update-slice, ...), channel_id=1, replica_groups=mesh['dp'=4,'fsdp'=8] {'fsdp'}, use_global_device_ids=true, to_apply=%add.3 | all-reduce | flops 6144 | bytes 24576
  54.8 12.8 %all-gather = bf16[8,1,384]{2,1,0:T(2,128)(2,1)S(1)} all-gather(bf16[1,1,384]{2,1,0:T(2,128)(2,1)S(1)} %reshape.219), channel_id=1, replica_groups=mesh['dp'=4,'fsdp'=8] {'fsdp'}, dimensions={0}, use_global_device_ids=true | all-gather | bytes 6912 | tf_op jit(solution)/shard_map/all_gather | solution.py:134
  68.9 8.7 %add_convert_fusion = bf16[4,282,2304]{2,1,0:T(8,128)(2,1)} fusion(f32[2304]{0:T(1024)S(1)} %maximum_convert_fusion, bf16[768,2304]{0,1:T(8,128)(2,1)} %all-gather.6.cloned.1.call-done, f32[768]{0:T(1024)S(1)} %convert_element_type.206, f32[768]{0:T(1024)S(1)} %convert_element_type.205, f32[4,282]{1,0:T(4,128)S(1)} %add_rsqrt_fusion.1, ...), kind=kOutput, calls=%fused_computation.95 | convolution fusion | flops 4002324480 | bytes 10493760 | tf_op jit(solution)/shard_map/bld,de->ble/dot_general | solution.py:20
  77.6 8.4 %copy.70 = bf16[4,282,2304]{1,2,0:T(8,128)(2,1)} copy(bf16[4,282,2304]{2,1,0:T(8,128)(2,1)} %add_convert_fusion) | data formatting | bytes 10395648 | tf_op jit(solution)/shard_map/convert_element_type | solution.py:120
  86.0 6.9 fusion.118
  94.7 20.8 %while.26 = (s32[]{:T(128)}, bf16[2,2,282,12,64]{2,4,3,1,0:T(8,128)(2,1)}, f32[2,2,12,282]{3,2,1,0:T(8,128)S(1)}, bf16[2,2,282,12,64]{2,4,3,1,0:T(8,128)(2,1)}, ...) while((s32[]{:T(128)}, ...), condition=%wide.region_5.6_spmd, body=%wide.region_2.5_spmd.sunk | while | flops 511925312 | bytes 37870064 | solution.py:126
  94.7 3.9 fusion.147
  101.1 4.0 fusion.149
  105.1 3.9 fusion.147
  111.5 4.0 fusion.149
  115.5 6.3 fusion.116
  124.1 6.6 all-gather.10.cloned.1.call-done
  130.7 14.2 %fusion.103 = (u8[282,3072]{1,0:T(8,128)(4,1)S(1)}, u8[282,3072]{1,0:T(8,128)(4,1)S(1)}, f32[4,282,3072]{2,1,0:T(8,128)S(1)}) fusion(f32[3072]{0:T(1024)S(1)} %bitcast.185, bf16[768,3072]{1,0:T(8,128)(2,1)} %all-gather.10.cloned.1.call-done, f32[4,282,768]{2,1,0:T(8,128)} %copy-done.9, f32[768]{0:T(1024)S(1)} %convert_element_type.213, ...), kind=kOutput, calls=%fused_computation.147 | convolution fusion | flops 5373683712 | bytes 23804736 | tf_op jit(solution)/shard_map/bld,df->blf/dot_general | solution.py:20
  144.9 5.0 copy-done.8
  150.0 33.6 %fusion.62 = bf16[4,282,3072]{2,1,0:T(8,128)(2,1)} fusion(f32[4,282,3072]{2,1,0:T(8,128)S(1)} %get-tuple-element.274, f32[3072]{0:T(1024)S(1)} %bitcast.186, u8[282,3072]{1,0:T(8,128)(4,1)S(1)} %get-tuple-element.172, u8[282,3072]{1,0:T(8,128)(4,1)S(1)} %get-tuple-element.171), kind=kLoop, calls=%fused_computation.69 | loop fusion | flops 246030336 | bytes 22536192 | tf_op jit(solution)/shard_map/convert_element_type | solution.py:142
  183.6 15.5 %convert_reduce_fusion = (f32[3072]{0:T(1024)}, bf16[4,282,3072]{2,1,0:T(8,128)(2,1)}) fusion(f32[4,282,3072]{2,1,0:T(8,128)} %copy-done.8, f32[3072]{0:T(1024)S(1)} %bitcast.187, bf16[3072,768]{1,0:T(8,128)(2,1)} %all-gather.12.cloned.1.call-done, f32[4]{0:T(128)S(1)} %copy-done.53, f32[4,282]{1,0:T(4,128)S(1)} %copy-done.25, bf16[4,282,768]{2,0,1:T(4,128)(2,1)} %param.37), kind=kOutput, calls=%fused_computation.81 | convolution fusion | flops 5371081728 | bytes 27271600 | tf_op jit(solution)/shard_map/bld,fd->blf/dot_general | solution.py:20
  199.1 11.5 %multiply_reduce_fusion.1 = (f32[768]{0:T(1024)}, f32[4,282]{1,0:T(4,128)S(1)}, f32[4,282]{1,0:T(4,128)S(1)}, f32[]{:T(128)}, f32[768]{0:T(1024)}, /*index=5*/f32[4,282,768]{2,1,0:T(8,128)S(1)}) fusion(f32[4,282,768]{2,1,0:T(8,128)S(1)} %copy-done.10, f32[4,282]{1,0:T(4,128)S(1)} %add_rsqrt_fusion, f32[4,282]{1,0:T(4,128)S(1)} %broadcast_multiply_fusion.4, ...), kind=kOutput, calls=%fused_computation.136 | convolution fusion | flops 5332963328 | bytes 18611236 | tf_op jit(solution)/shard_map/blf,df->bld/dot_general | solution.py:20
  210.7 11.4 %fusion.97 = (f32[]{:T(128)}, f32[768]{0:T(1024)}, f32[]{:T(128)}, bf16[4,282,768]{2,1,0:T(8,128)(2,1)}, f32[768]{0:T(1024)}, /*index=5*/bf16[4,282,768]{2,1,0:T(8,128)(2,1)}) fusion(f32[4,282,768]{2,1,0:T(8,128)} %get-tuple-element.273, f32[768]{0:T(1024)S(1)} %convert_element_type.211, f32[4,282]{1,0:T(4,128)S(1)} %copy-done.25, ...), kind=kOutput, calls=%fused_computation.130 | convolution fusion | flops 5348558848 | bytes 27280456 | tf_op jit(solution)/shard_map/blf,fd->bld/dot_general | solution.py:20
  222.1 5.3 convolution_bitcast_fusion.3
  227.4 4.6 convolution_convert_fusion
  231.9 4.0 copy.73
  241.4 45.2 %while.27 = (s32[]{:T(128)}, bf16[2,2,282,12,64]{2,4,3,1,0:T(8,128)(2,1)}, bf16[2,2,282,12,64]{2,4,3,1,0:T(8,128)(2,1)}, bf16[2,2,282,12,64]{2,4,3,1,0:T(8,128)(...) while((s32[]{:T(128)}, ...), condition=%wide.region_12.13_spmd, body=%wide.region_10.12_spmd.sunk | while | flops 1252276864 | bytes 94541240 | solution.py:181
  241.4 2.9 fusion.158
  244.3 5.6 multiply_reduce_fusion.7
  249.9 3.4 multiply_convert_fusion.10
  253.3 4.4 fusion.160
  260.4 3.6 fusion.161
  264.0 2.9 fusion.158
  266.9 5.6 multiply_reduce_fusion.7
  272.5 3.4 multiply_convert_fusion.10
  275.9 4.4 fusion.160
  283.0 3.6 fusion.161
  286.6 2.8 copy.74
  289.5 4.3 copy.75
  293.8 4.3 copy.76
  298.2 10.0 %convolution_bitcast_fusion.2 = f32[768,2304]{0,1:T(8,128)} fusion(bf16[4,282,768]{2,1,0:T(8,128)(2,1)} %copy.76, bf16[4,282,768]{2,1,0:T(8,128)(2,1)} %copy.75, bf16[4,282,768]{2,1,0:T(8,128)(2,1)S(1)} %copy.74, f32[768]{0:T(1024)S(1)} %copy-done.39, f32[768]{0:T(1024)S(1)} %copy-done.32, f32[4,282]{1,0:T(4,128)S(1)} %copy-done.22, ...), kind=kOutput, calls=%fused_computation.98 | convolution fusion | flops 4012720128 | bytes 14023488 | tf_op jit(solution)/shard_map/bld,ble->de/dot_general | solution.py:20
  308.9 12.6 %convolution_bitcast_fusion.1 = f32[768,3072]{1,0:T(8,128)} fusion(bf16[4,282,3072]{2,1,0:T(8,128)(2,1)} %get-tuple-element.278, f32[4,282,768]{2,1,0:T(8,128)} %copy-done.9, f32[768]{0:T(1024)S(1)} %copy-done.41, f32[768]{0:T(1024)S(1)} %copy-done.34, f32[4,282]{1,0:T(4,128)S(1)} %copy-done.24, f32[4,282]{1,0:T(4,128)S(1)} %copy-done.20), kind=kOutput, calls=%fused_computation.97 | convolution fusion | flops 5326903296 | bytes 19848000 | tf_op jit(solution)/shard_map/bld,blf->df/dot_general | solution.py:20
  322.2 12.0 %convolution_bitcast_fusion = f32[3072,768]{1,0:T(8,128)} fusion(bf16[4,282,3072]{2,1,0:T(8,128)(2,1)} %fusion.62, f32[4]{0:T(128)S(1)} %copy-done.54, f32[4,282]{1,0:T(4,128)S(1)} %copy-done.26, bf16[4,282,768]{2,0,1:T(4,128)(2,1)} %param.37), kind=kOutput, calls=%fused_computation.96 | convolution fusion | flops 5326036992 | bytes 18104752 | tf_op jit(solution)/shard_map/blf,bld->fd/dot_general | solution.py:20
  336.3 9.6 %fusion.94 = (f32[768]{0:T(1024)S(1)}, f32[4,282]{1,0:T(4,128)}, f32[4,282]{1,0:T(4,128)}, f32[768]{0:T(1024)}, f32[4,282,768]{2,1,0:T(8,128)}) fusion(f32[4,282]{1,0:T(4,128)S(1)} %copy-done.22, f32[4,282]{1,0:T(4,128)S(1)} %copy-done.18, bf16[4,282,768]{2,0,1:T(4,128)(2,1)S(1)} %copy-done.6, f32[768]{0:T(1024)S(1)} %copy-done.32, ...), kind=kOutput, calls=%fused_computation.127 | convolution fusion | flops 4016181760 | bytes 13961856 | tf_op jit(solution)/shard_map/ble,de->bld/dot_general | solution.py:20
  347.7 36.8 %reduce-scatter.5.cloned.1.call-done = f32[768,288]{0,1:T(8,128)} async-done(((f32[768,2304]{0,1:T(8,128)}), f32[768,288]{0,1:T(8,128)}) %reduce-scatter.5.cloned.1.call-update) | async-done | bytes 884752 | tf_op jit(solution)/shard_map/reduce_scatter | solution.py:199
  386.5 98.2 %reduce-scatter.9.cloned.1.call-done = f32[768,384]{1,0:T(8,128)} async-done(((f32[768,3072]{1,0:T(8,128)}), f32[768,384]{1,0:T(8,128)}) %reduce-scatter.9.cloned.1.call-update) | async-done | bytes 1179664 | tf_op jit(solution)/shard_map/reduce_scatter | solution.py:172
  486.9 98.1 %reduce-scatter.11.cloned.1.call-done = f32[384,768]{1,0:T(8,128)} async-done(((f32[3072,768]{1,0:T(8,128)}), f32[384,768]{1,0:T(8,128)}) %reduce-scatter.11.cloned.1.call-update) | async-done | bytes 1179664 | tf_op jit(solution)/shard_map/reduce_scatter | solution.py:174
  587.6 38.5 %all-reduce.17 = (f32[1]{0:T(128)}, f32[1]{0:T(128)}, f32[1]{0:T(128)}, f32[]{:T(128)}) all-reduce(f32[1]{0:T(128)} %bitcast.43, f32[1]{0:T(128)} %bitcast.42, f32[1]{0:T(128)} %bitcast.41, f32[]{:T(128)} %fusion.112), channel_id=1, replica_groups=mesh['dp'=4,'fsdp'=8] {'dp','fsdp'}, use_global_device_ids=true, to_apply=%region_55.56 | all-reduce | flops 4 | bytes 32 | tf_op jit(solution)/shard_map/psum | solution.py:145
  628.5 27.3 %all-reduce.18 = (bf16[768]{0:T(1024)(128)(2,1)S(1)}, bf16[768]{0:T(1024)(128)(2,1)S(1)}, bf16[768]{0:T(1024)(128)(2,1)S(1)}, bf16[768]{0:T(1024)(128)(2,1)S(1)}...) all-reduce(f32[768]{0:T(1024)S(1)} %get-tuple-element.175, ...), channel_id=2, replica_groups=mesh['dp'=4,'fsdp'=8] {'fsdp'}, use_global_device_ids=true, to_apply=%region_16.17.clone | all-reduce | flops 9216 | bytes 55296
  656.5 10.0 %all-reduce.20 = (bf16[96]{0:T(256)(128)(2,1)S(1)}, bf16[96]{0:T(256)(128)(2,1)S(1)}, bf16[96]{0:T(256)(128)(2,1)S(1)}, bf16[96]{0:T(256)(128)(2,1)S(1)}, bf16[9...) all-reduce(bf16[96]{0:T(256)(128)(2,1)S(1)} %dynamic-slice.43, ...), channel_id=1, replica_groups=mesh['dp'=4,'fsdp'=8] {'dp'}, use_global_device_ids=true, to_apply=%region_17.18 | all-reduce | flops 1152 | bytes 4608 | tf_op jit(solution)/shard_map/psum | solution.py:206
  671.2 6.1 fusion.93
  677.4 4.0 copy.79
  681.4 2.5 copy.78
  (235 shorter events, 63.2 us)
Async XLA Ops:
  7.2 45.0 %copy-start.5 = (bf16[4,282,768]{2,0,1:T(4,128)(2,1)S(1)}, bf16[4,282,768]{2,0,1:T(4,128)(2,1)}, u32[]{:S(2)}) copy-start(bf16[4,282,768]{2,0,1:T(4,128)(2,1)} %param.21) | copy-start | bytes 5197828
  7.2 46.2 %copy-start.50 = (s32[4,2]{0,1:T(2,128)S(1)}, s32[4,2]{0,1:T(2,128)}, u32[]{:S(2)}) copy-start(s32[4,2]{0,1:T(2,128)} %param.22) | copy-start | bytes 100
  7.2 47.0 %copy-start.51 = (s32[4,2]{0,1:T(2,128)S(1)}, s32[4,2]{0,1:T(2,128)}, u32[]{:S(2)}) copy-start(s32[4,2]{0,1:T(2,128)} %param.23) | copy-start | bytes 100
  7.2 47.5 %copy-start.52 = (bf16[384]{0:T(512)(128)(2,1)S(1)}, bf16[384]{0:T(512)(128)(2,1)}, u32[]{:S(2)}) copy-start(bf16[384]{0:T(512)(128)(2,1)} %param.34) | copy-start | bytes 2308
  7.2 61.6 %all-gather.6.cloned.1.call-start = ((), (), s32[]{:S(2)}) async-start(), calls=%async_computation.4 | async-start | bytes 3981312 | tf_op jit(solution)/shard_map/all_gather | solution.py:107
  8.0 107.5 %all-gather.8.cloned.1.call-start = ((), (), s32[]{:S(2)}) async-start(), calls=%async_computation.5 | async-start | bytes 1327104 | tf_op jit(solution)/shard_map/all_gather | solution.py:110
  8.7 122.0 %all-gather.10.cloned.1.call-start = ((), (), s32[]{:S(2)}) async-start(), calls=%async_computation.6 | async-start | bytes 5308416 | tf_op jit(solution)/shard_map/all_gather | solution.py:133
  9.4 174.1 %all-gather.12.cloned.1.call-start = ((), (), s32[]{:S(2)}) async-start(), calls=%async_computation.7 | async-start | bytes 5308416 | tf_op jit(solution)/shard_map/all_gather | solution.py:135
  10.0 335.9 %reduce-scatter.7.cloned.1.call-start = ((), (), s32[]{:S(2)}) async-start(), calls=%async_computation.9 | async-start | bytes 2654208 | tf_op jit(solution)/shard_map/reduce_scatter | solution.py:202
  50.3 27.2 %copy-start.31 = (f32[768]{0:T(1024)}, f32[768]{0:T(1024)S(1)}, u32[]{:S(2)}) copy-start(f32[768]{0:T(1024)S(1)} %convert_element_type.205) | copy-start | bytes 9220
  50.4 27.2 %copy-start.38 = (f32[768]{0:T(1024)}, f32[768]{0:T(1024)S(1)}, u32[]{:S(2)}) copy-start(f32[768]{0:T(1024)S(1)} %convert_element_type.206) | copy-start | bytes 9220
  52.2 25.4 %copy-start.17 = (f32[4,282]{1,0:T(4,128)}, f32[4,282]{1,0:T(4,128)S(1)}, u32[]{:S(2)}) copy-start(f32[4,282]{1,0:T(4,128)S(1)} %broadcast_multiply_fusion.5) | copy-start | bytes 13540
  52.8 24.8 %copy-start.21 = (f32[4,282]{1,0:T(4,128)}, f32[4,282]{1,0:T(4,128)S(1)}, u32[]{:S(2)}) copy-start(f32[4,282]{1,0:T(4,128)S(1)} %add_rsqrt_fusion.1) | copy-start | bytes 13540
  54.0 23.6 %copy-start.48 = (s32[4,1]{0,1:T(1,128)}, s32[4,1]{0,1:T(1,128)S(1)}, u32[]{:S(2)}) copy-start(s32[4,1]{0,1:T(1,128)S(1)} %get-tuple-element.258) | copy-start | bytes 52
  54.7 155.9 %copy-start.33 = (f32[768]{0:T(1024)}, f32[768]{0:T(1024)S(1)}, u32[]{:S(2)}) copy-start(f32[768]{0:T(1024)S(1)} %convert_element_type.212) | copy-start | bytes 9220
  54.7 76.0 %copy-start.40 = (f32[768]{0:T(1024)}, f32[768]{0:T(1024)S(1)}, u32[]{:S(2)}) copy-start(f32[768]{0:T(1024)S(1)} %convert_element_type.213) | copy-start | bytes 9220
  121.8 88.8 %copy-start.19 = (f32[4,282]{1,0:T(4,128)}, f32[4,282]{1,0:T(4,128)S(1)}, u32[]{:S(2)}) copy-start(f32[4,282]{1,0:T(4,128)S(1)} %broadcast_multiply_fusion.4) | copy-start | bytes 13540
  124.1 86.5 %copy-start.23 = (f32[4,282]{1,0:T(4,128)}, f32[4,282]{1,0:T(4,128)S(1)}, u32[]{:S(2)}) copy-start(f32[4,282]{1,0:T(4,128)S(1)} %add_rsqrt_fusion) | copy-start | bytes 13540
  150.0 33.6 %copy-start.25 = (f32[4,282]{1,0:T(4,128)S(1)}, f32[4,282]{1,0:T(4,128)}, u32[]{:S(2)}) copy-start(f32[4,282]{1,0:T(4,128)} %fusion.111) | copy-start | bytes 13540
  150.0 33.6 %copy-start.53 = (f32[4]{0:T(128)S(1)}, f32[4]{0:T(128)}, u32[]{:S(2)}) copy-start(f32[4]{0:T(128)} %get-tuple-element.269) | copy-start | bytes 52
  183.6 15.5 %copy-start.10 = (f32[4,282,768]{2,1,0:T(8,128)S(1)}, f32[4,282,768]{2,1,0:T(8,128)}, u32[]{:S(2)}) copy-start(f32[4,282,768]{2,1,0:T(8,128)} %copy-done.9) | copy-start | bytes 10395652
  199.1 11.6 %copy-start.11 = (bf16[4,282,3072]{2,1,0:T(8,128)(2,1)S(1)}, bf16[4,282,3072]{2,1,0:T(8,128)(2,1)}, u32[]{:S(2)}) copy-start(bf16[4,282,3072]{2,1,0:T(8,128)(2,1)} %fusion.62) | copy-start | bytes 20791300
  199.1 11.6 %copy-start.14 = (bf16[4,282,768]{2,0,1:T(4,128)(2,1)S(1)}, bf16[4,282,768]{2,0,1:T(4,128)(2,1)}, u32[]{:S(2)}) copy-start(bf16[4,282,768]{2,0,1:T(4,128)(2,1)} %param.37) | copy-start | bytes 5197828
  199.1 11.6 %copy-start.42 = (f32[768]{0:T(1024)S(1)}, f32[768]{0:T(1024)}, u32[]{:S(2)}) copy-start(f32[768]{0:T(1024)} %convert_element_type.217) | copy-start | bytes 9220
  199.1 11.6 %copy-start.55 = (bf16[3072,768]{1,0:T(8,128)(2,1)S(1)}, bf16[3072,768]{1,0:T(8,128)(2,1)}, u32[]{:S(2)}) copy-start(bf16[3072,768]{1,0:T(8,128)(2,1)} %all-gather.12.cloned.1.call-done) | copy-start | bytes 14155780
  210.6 11.5 %copy-start.12 = (f32[4,282,768]{2,1,0:T(8,128)}, f32[4,282,768]{2,1,0:T(8,128)S(1)}, u32[]{:S(2)}) copy-start(f32[4,282,768]{2,1,0:T(8,128)S(1)} %get-tuple-element.275) | copy-start | bytes 10395652
  210.6 11.5 %copy-start.27 = (f32[4,282]{1,0:T(4,128)}, f32[4,282]{1,0:T(4,128)S(1)}, u32[]{:S(2)}) copy-start(f32[4,282]{1,0:T(4,128)S(1)} %get-tuple-element.279) | copy-start | bytes 13540
  210.6 11.5 %copy-start.29 = (f32[4,282]{1,0:T(4,128)}, f32[4,282]{1,0:T(4,128)S(1)}, u32[]{:S(2)}) copy-start(f32[4,282]{1,0:T(4,128)S(1)} %get-tuple-element.280) | copy-start | bytes 13540
  236.0 148.5 %reduce-scatter.5.cloned.1.call-start = ((), (), s32[]{:S(2)}) async-start(), calls=%async_computation.8 | async-start | bytes 7962624 | tf_op jit(solution)/shard_map/reduce_scatter | solution.py:199
  289.5 8.7 %copy-start.6 = (bf16[4,282,768]{2,0,1:T(4,128)(2,1)S(1)}, bf16[4,282,768]{2,0,1:T(4,128)(2,1)}, u32[]{:S(2)}) copy-start(bf16[4,282,768]{2,0,1:T(4,128)(2,1)} %param.21) | copy-start | bytes 5197828
  289.5 8.7 %copy-start.18 = (f32[4,282]{1,0:T(4,128)S(1)}, f32[4,282]{1,0:T(4,128)}, u32[]{:S(2)}) copy-start(f32[4,282]{1,0:T(4,128)} %copy-done.17) | copy-start | bytes 13540
  289.5 8.7 %copy-start.22 = (f32[4,282]{1,0:T(4,128)S(1)}, f32[4,282]{1,0:T(4,128)}, u32[]{:S(2)}) copy-start(f32[4,282]{1,0:T(4,128)} %copy-done.21) | copy-start | bytes 13540
  289.5 8.7 %copy-start.32 = (f32[768]{0:T(1024)S(1)}, f32[768]{0:T(1024)}, u32[]{:S(2)}) copy-start(f32[768]{0:T(1024)} %copy-done.31) | copy-start | bytes 9220
  308.2 176.5 %reduce-scatter.9.cloned.1.call-start = ((), (), s32[]{:S(2)}) async-start(), calls=%async_computation.10 | async-start | bytes 10616832 | tf_op jit(solution)/shard_map/reduce_scatter | solution.py:172
  321.5 263.4 %reduce-scatter.11.cloned.1.call-start = ((), (), s32[]{:S(2)}) async-start(), calls=%async_computation.11 | async-start | bytes 10616832 | tf_op jit(solution)/shard_map/reduce_scatter | solution.py:174
  334.2 352.7 %all-reduce.24.cloned.1.call-start = ((), (), s32[]{:S(2)}) async-start(), calls=%async_computation.12 | async-start | bytes 3538944 | tf_op jit(solution)/shard_map/psum | solution.py:208
  345.9 241.3 %copy-start.4 = (bf16[2,2,282,12,64]{2,4,3,1,0:T(8,128)(2,1)S(1)}, bf16[2,2,282,12,64]{2,4,3,1,0:T(8,128)(2,1)}, u32[]{:S(2)}) copy-start(bf16[2,2,282,12,64]{2,4,3,1,0:T(8,128)(2,1)} %get-tuple-element.110) | copy-start | bytes 5197828
  587.1 41.4 %copy-start.35 = (f32[3072]{0:T(1024)S(1)}, f32[3072]{0:T(1024)}, u32[]{:S(2)}) copy-start(f32[3072]{0:T(1024)} %get-tuple-element.277) | copy-start | bytes 36868
  587.1 41.4 %copy-start.43 = (f32[768]{0:T(1024)S(1)}, f32[768]{0:T(1024)}, u32[]{:S(2)}) copy-start(f32[768]{0:T(1024)} %get-tuple-element.173) | copy-start | bytes 9220
  587.1 41.4 %copy-start.44 = (f32[768]{0:T(1024)S(1)}, f32[768]{0:T(1024)}, u32[]{:S(2)}) copy-start(f32[768]{0:T(1024)} %get-tuple-element.180) | copy-start | bytes 9220
  587.1 41.4 %copy-start.45 = (f32[768]{0:T(1024)S(1)}, f32[768]{0:T(1024)}, u32[]{:S(2)}) copy-start(f32[768]{0:T(1024)} %get-tuple-element.183) | copy-start | bytes 9220
  587.1 41.4 %copy-start.46 = (f32[768]{0:T(1024)S(1)}, f32[768]{0:T(1024)}, u32[]{:S(2)}) copy-start(f32[768]{0:T(1024)} %get-tuple-element.267) | copy-start | bytes 9220
  587.1 41.4 %copy-start.47 = (f32[768]{0:T(1024)S(1)}, f32[768]{0:T(1024)}, u32[]{:S(2)}) copy-start(f32[768]{0:T(1024)} %get-tuple-element.181) | copy-start | bytes 9220
  587.1 84.1 %copy-start.37 = (f32[4,282]{1,0:T(4,128)S(1)}, f32[4,282]{1,0:T(4,128)}, u32[]{:S(2)}) copy-start(f32[4,282]{1,0:T(4,128)} %get-tuple-element.176) | copy-start | bytes 13540
  587.1 84.1 %copy-start.36 = (f32[4,282]{1,0:T(4,128)S(1)}, f32[4,282]{1,0:T(4,128)}, u32[]{:S(2)}) copy-start(f32[4,282]{1,0:T(4,128)} %get-tuple-element.177) | copy-start | bytes 13540
  587.1 84.1 %copy-start.28 = (f32[4,282]{1,0:T(4,128)S(1)}, f32[4,282]{1,0:T(4,128)}, u32[]{:S(2)}) copy-start(f32[4,282]{1,0:T(4,128)} %copy-done.27) | copy-start | bytes 13540
  587.1 84.1 %copy-start.30 = (f32[4,282]{1,0:T(4,128)S(1)}, f32[4,282]{1,0:T(4,128)}, u32[]{:S(2)}) copy-start(f32[4,282]{1,0:T(4,128)} %copy-done.29) | copy-start | bytes 13540
  587.6 83.6 %copy-start.7 = (bf16[4,282,768]{2,0,1:T(4,128)(2,1)S(1)}, bf16[4,282,768]{2,0,1:T(4,128)(2,1)}, u32[]{:S(2)}) copy-start(bf16[4,282,768]{2,0,1:T(4,128)(2,1)} %param.21) | copy-start | bytes 5197828
  (21 other events, 56.7 us)
Sparse Core Ops, SparseCore 0:
  9.7 44.8 all-gather.5
  56.2 21.5 all-gather.7
  79.4 51.2 all-gather.9
  132.2 50.4 all-gather.11
  236.1 34.8 reduce-scatter.6
  308.4 76.1 reduce-scatter.4
  386.8 97.8 reduce-scatter.8
  487.0 97.8 reduce-scatter.10
  589.5 63.2 all-reduce.23
where the time goes:
time: 705 us; the launch traced here: 700 us
  waiting for transfers between devices  242 us (34%)
  matrix products  173 us (25%)
  blocking collectives  120 us (17%)
  other arithmetic  81 us (11%)
  local copies, waits for them, and re-layouts  65.5 us (9%)
  between operations  17.3 us (2%)
    dot_general x26, matrix products, product(): return jnp.einsum(formula, left, right, preferred_element_type=jnp.float32)  173 us
    reduce_scatter x1, waiting for transfers between devices, shards(): lax.psum_scatter(grad_up_weight, 'fsdp', scatter_dimension=1, tiled=True)  98.2 us
    reduce_scatter x1, waiting for transfers between devices, shards(): lax.psum_scatter(grad_down_weight, 'fsdp', scatter_dimension=0, tiled=True)  98.1 us
    unnamed x2, blocking collectives  58.9 us
    psum x1, blocking collectives, shards(): lax.psum((jnp.sum(row_mask * middle * middle), jnp.sum(row_mask * attn_ou...  38.5 us
    reduce_scatter x1, waiting for transfers between devices, shards(): lax.psum_scatter(grad_attend_weight, 'fsdp', scatter_dimension=1, tiled=T...  36.8 us
    convert_element_type x1, other arithmetic, shards(): activated = jax.nn.gelu(hidden_pre, approximate=False).astype(jnp.bfloat16)  33.6 us
    unnamed x134, local copies, waits for them, and re-layouts  23.5 us
  transfers between devices with their start and end apart: 9, of which 4 were waited for; matrix products, arithmetic and copies ran while one was open for 35% of the time, Pallas kernels for 0%

commit v1 on v0

v1 whole, which is shorter than its diff:
```python
import functools

import jax
import jax.numpy as jnp
from jax import lax
from jax.experimental import pallas as pl
from jax.experimental.pallas import tpu as pltpu
from jax.sharding import PartitionSpec as P

HEAD_DIM = 64
EPS = 1e-06
KEEP_PROB = 0.9
MASKED = -1e30
INV_ROOT_TWO = 0.7071067811865476
INV_ROOT_TWO_PI = 0.3989422804014327
F32 = jnp.float32
BF16 = jnp.bfloat16
MIB = 1024 * 1024


def nn(left, right):
    return lax.dot_general(left, right, (((1,), (0,)), ((), ())), preferred_element_type=F32)


def nt(left, right):
    return lax.dot_general(left, right, (((1,), (1,)), ((), ())), preferred_element_type=F32)


def tn(left, right):
    return lax.dot_general(left, right, (((0,), (0,)), ((), ())), preferred_element_type=F32)


def mean_row(values):
    return jnp.sum(values, -1, keepdims=True) * (1.0 / values.shape[-1])


def normalize(values):
    center = values - mean_row(values)
    rstd = lax.rsqrt(mean_row(center * center) + EPS)
    return center * rstd, rstd


def col_sum(values):
    return jnp.sum(values, 0, keepdims=True)


def params(limit, steps=1):
    return pltpu.CompilerParams(
        dimension_semantics=("arbitrary",) * steps, vmem_limit_bytes=limit * MIB
    )


def whole(shape, buffers=1):
    zeros = (0,) * len(shape)
    return pl.BlockSpec(shape, lambda *_: zeros, pipeline_mode=pl.Buffered(buffers))


def by_image(shape):
    rest = (0,) * len(shape)
    return pl.BlockSpec((1,) + shape, lambda i, *_: (i,) + rest)


SMEM = pl.BlockSpec(memory_space=pltpu.SMEM)


def front_kernel(seq, pad, counts, depth, x_ref, cot_ref, w_ref, gain_ref, shift_ref, bias_ref,
                 a1_ref, gm_ref, qkv_ref, o_ref, lse_ref, xs, lse_s):
    i = pl.program_id(0)
    width = x_ref.shape[-1]
    pairs = width // 128
    count = counts[i]
    rows = lax.broadcasted_iota(jnp.int32, (pad, 1), 0)
    xs[pad - 8:pad, :] = jnp.zeros((8, width), F32)
    xs[0:seq, :] = cot_ref[0].astype(F32)
    gm_ref[0] = jnp.where(rows < count, xs[...] * depth[i, 1], 0.0).astype(BF16)
    xs[0:seq, :] = x_ref[0].astype(F32)
    normed, _ = normalize(xs[...])
    a1 = (normed * gain_ref[...] + shift_ref[...]).astype(BF16)
    a1_ref[0] = a1
    for c in range(0, 3 * width, 384):
        qkv_ref[0, :, c:c + 384] = (nt(a1, w_ref[c:c + 384, :]) + bias_ref[:, c:c + 384]).astype(BF16)
    ok = lax.broadcasted_iota(jnp.int32, (pad, pad), 1) < count
    lane = lax.broadcasted_iota(jnp.int32, (pad, 128), 1)
    lse_s[...] = jnp.zeros((pad, 128), F32)

    def pair(p):
        at = pl.multiple_of(p * 128, 128)
        q = qkv_ref[0, :, pl.ds(at, 128)] * 0.125
        k = qkv_ref[0, :, pl.ds(width + at, 128)]
        v = qkv_ref[0, :, pl.ds(2 * width + at, 128)]
        total = jnp.zeros((pad, 128), F32)
        for half in range(2):
            mine = (lane >= 64) if half else (lane < 64)
            scores = jnp.where(ok, nt(jnp.where(mine, q, 0), k), MASKED)
            top = jnp.max(scores, -1, keepdims=True)
            e = jnp.exp(scores - top)
            s = jnp.sum(e, -1, keepdims=True)
            prob = (e * (1.0 / s)).astype(BF16)
            total = total + nn(prob, jnp.where(mine, v, 0))
            lse_s[...] = jnp.where(lane == 2 * p + half, top + jnp.log(s), lse_s[...])
        o_ref[0, :, pl.ds(at, 128)] = total.astype(BF16)

    for p in range(pairs):
        pair(p)
    lse_ref[0] = jnp.transpose(lse_s[...])[0:16, :]


def front(counts, depth, images, cot, w, gain, shift, bias, pad):
    n, seq, width = images.shape
    grid_spec = pltpu.PrefetchScalarGridSpec(
        num_scalar_prefetch=2,
        grid=(n,),
        in_specs=[
            by_image((seq, width)), by_image((seq, width)),
            whole(w.shape), whole(gain.shape), whole(shift.shape), whole(bias.shape),
        ],
        out_specs=[
            by_image((pad, width)), by_image((pad, width)), by_image((pad, 3 * width)),
            by_image((pad, width)), by_image((16, pad)),
        ],
        scratch_shapes=[pltpu.VMEM((pad, width), F32), pltpu.VMEM((pad, 128), F32)],
    )
    return pl.pallas_call(
        functools.partial(front_kernel, seq, pad),
        out_shape=[
            jax.ShapeDtypeStruct((n, pad, width), BF16),
            jax.ShapeDtypeStruct((n, pad, width), BF16),
            jax.ShapeDtypeStruct((n, pad, 3 * width), BF16),
            jax.ShapeDtypeStruct((n, pad, width), BF16),
            jax.ShapeDtypeStruct((n, 16, pad), F32),
        ],
        grid_spec=grid_spec,
        compiler_params=params(40),
        cost_estimate=pl.CostEstimate(
            flops=2 * n * pad * width * (3 * width + 4 * pad), bytes_accessed=20 * MIB,
            transcendentals=n * 12 * pad * pad),
        name="front",
    )(counts, depth, images, cot, w, gain, shift, bias)


def middle_kernel(seq, pad, counts, depth, o_ref, x_ref, w_ref, bias_ref, gain_ref, shift_ref,
                  x1_ref, a2_ref, sums_ref, xs):
    i = pl.program_id(0)
    width = x_ref.shape[-1]
    rows = lax.broadcasted_iota(jnp.int32, (pad, 1), 0)
    ok = rows < counts[i]
    xs[pad - 8:pad, :] = jnp.zeros((8, width), F32)
    xs[0:seq, :] = x_ref[0].astype(F32)
    attn = nn(o_ref[0], w_ref[...]) + bias_ref[...]
    x1 = xs[...] + depth[i, 0] * attn
    x1_ref[0] = x1
    sums_ref[0, 0:1, :] = col_sum(jnp.where(ok, x1 * x1, 0.0))
    sums_ref[0, 1:2, :] = col_sum(jnp.where(ok, attn * attn, 0.0))
    sums_ref[0, 2:8, :] = jnp.zeros((6, width), F32)
    normed, _ = normalize(x1)
    a2_ref[0] = (normed * gain_ref[...] + shift_ref[...]).astype(BF16)


def middle(counts, depth, o, images, w, bias, gain, shift, pad):
    n, seq, width = images.shape
    grid_spec = pltpu.PrefetchScalarGridSpec(
        num_scalar_prefetch=2,
        grid=(n,),
        in_specs=[
            by_image((pad, width)), by_image((seq, width)),
            whole(w.shape), whole(bias.shape), whole(gain.shape), whole(shift.shape),
        ],
        out_specs=[by_image((pad, width)), by_image((pad, width)), by_image((8, width))],
        scratch_shapes=[pltpu.VMEM((pad, width), F32)],
    )
    return pl.pallas_call(
        functools.partial(middle_kernel, seq, pad),
        out_shape=[
            jax.ShapeDtypeStruct((n, pad, width), F32),
            jax.ShapeDtypeStruct((n, pad, width), BF16),
            jax.ShapeDtypeStruct((n, 8, width), F32),
        ],
        grid_spec=grid_spec,
        compiler_params=params(24),
        cost_estimate=pl.CostEstimate(
            flops=2 * n * pad * width * width, bytes_accessed=10 * MIB, transcendentals=0),
        name="middle",
    )(counts, depth, o, images, w, bias, gain, shift)


def gelu_pair(u):
    size = jnp.abs(u)
    t = 1.0 / (1.0 + (0.3275911 * INV_ROOT_TWO) * size)
    bell = jnp.exp(-0.5 * (u * u))
    series = t * (0.5 * 0.254829592 + t * (0.5 * -0.284496736 + t * (
        0.5 * 1.421413741 + t * (0.5 * -1.453152027 + t * (0.5 * 1.061405429)))))
    tail = series * bell
    phi = jnp.where(u >= 0, 1.0 - tail, tail)
    return u * phi, phi + u * (bell * INV_ROOT_TWO_PI)


def feed_kernel(seq, pad, counts, depth, a2_ref, gm_ref, up_ref, down_ref, bu_ref, x1_ref, cot_ref,
                bd_ref, gain_ref,
                dup_ref, ddown_ref, gbu_ref, y_ref, gx_ref, ga_ref, vec_ref,
                a2t, gmt, mlp, ga2, hs, gus, cs):
    j = pl.program_id(0)
    n = x1_ref.shape[0]

    @pl.when(j == 0)
    def _():
        a2t[...] = jnp.transpose(a2_ref[...])
        gmt[...] = jnp.transpose(gm_ref[...])
        mlp[...] = jnp.zeros_like(mlp)
        ga2[...] = jnp.zeros_like(ga2)

    gbu = jnp.zeros(bu_ref.shape[1:], F32)
    for i in range(n):
        at = slice(i * pad, (i + 1) * pad)
        u = nt(a2_ref[at, :], up_ref[...]) + bu_ref[0]
        t = nt(gm_ref[at, :], down_ref[...])
        act, slope = gelu_pair(u)
        h = act.astype(BF16)
        gu = (t * slope).astype(BF16)
        hs[at, :] = h
        gus[at, :] = gu
        gbu = gbu + col_sum(gu.astype(F32))
        mlp[at, :] += nn(h, down_ref[...])
        ga2[at, :] += nn(gu, up_ref[...])
    gbu_ref[0] = gbu
    dup_ref[0] = nn(a2t[...], gus[...]).astype(BF16)
    ddown_ref[0] = nn(gmt[...], hs[...]).astype(BF16)

    @pl.when(j == pl.num_programs(0) - 1)
    def _():
        width = x1_ref.shape[-1]
        rows = lax.broadcasted_iota(jnp.int32, (pad, 1), 0)
        cs[pad - 8:pad, :] = jnp.zeros((8, width), F32)
        msum = jnp.zeros((1, width), F32)
        ggain = jnp.zeros((1, width), F32)
        gshift = jnp.zeros((1, width), F32)
        gdown = jnp.zeros((1, width), F32)
        gout = jnp.zeros((1, width), F32)
        for i in range(n):
            at = slice(i * pad, (i + 1) * pad)
            ok = rows < counts[i]
            x1 = x1_ref[i]
            out = mlp[at, :] + bd_ref[...]
            msum = msum + col_sum(jnp.where(ok, out * out, 0.0))
            y_ref[i] = jnp.where(ok, x1 + depth[i, 1] * out, 0.0).astype(BF16)[0:seq]
            cs[0:seq, :] = cot_ref[i].astype(F32)
            g = jnp.where(ok, cs[...], 0.0)
            gdown = gdown + col_sum(gm_ref[at, :].astype(F32))
            back = ga2[at, :]
            normed, rstd = normalize(x1)
            ggain = ggain + col_sum(back * normed)
            gshift = gshift + col_sum(back)
            e = back * gain_ref[...]
            gx = g + rstd * (e - mean_row(e) - normed * mean_row(e * normed))
            gx_ref[i] = gx
            ga = (depth[i, 0] * gx).astype(BF16)
            ga_ref[i] = ga
            gout = gout + col_sum(ga.astype(F32))
        vec_ref[0:1, :] = ggain
        vec_ref[1:2, :] = gshift
        vec_ref[2:3, :] = gdown
        vec_ref[3:4, :] = gout
        vec_ref[4:5, :] = msum
        vec_ref[5:8, :] = jnp.zeros((3, width), F32)


def feed(counts, depth, a2, gm, up, down, bu, x1, cot, bd, gain, seq, pad, block):
    rows, width = a2.shape
    n = rows // pad
    hidden = up.shape[0]
    steps = hidden // block
    at = lambda j, *_: (j, 0)
    at3 = lambda j, *_: (j, 0, 0)
    grid_spec = pltpu.PrefetchScalarGridSpec(
        num_scalar_prefetch=2,
        grid=(steps,),
        in_specs=[
            whole(a2.shape), whole(gm.shape),
            pl.BlockSpec((block, width), at), pl.BlockSpec((block, width), at),
            pl.BlockSpec((1, 1, block), at3),
            whole(x1.shape), whole(cot.shape), whole(bd.shape), whole(gain.shape),
        ],
        out_specs=[
            pl.BlockSpec((1, width, block), at3), pl.BlockSpec((1, width, block), at3),
            pl.BlockSpec((1, 1, block), at3),
            whole((n, seq, width)), whole((n, pad, width)), whole((n, pad, width)), whole((8, width)),
        ],
        scratch_shapes=[
            pltpu.VMEM((width, rows), BF16), pltpu.VMEM((width, rows), BF16),
            pltpu.VMEM((rows, width), F32), pltpu.VMEM((rows, width), F32),
            pltpu.VMEM((rows, block), BF16), pltpu.VMEM((rows, block), BF16),
            pltpu.VMEM((pad, width), F32),
        ],
    )
    return pl.pallas_call(
        functools.partial(feed_kernel, seq, pad),
        out_shape=[
            jax.ShapeDtypeStruct((steps, width, block), BF16),
            jax.ShapeDtypeStruct((steps, width, block), BF16),
            jax.ShapeDtypeStruct((steps, 1, block), F32),
            jax.ShapeDtypeStruct((n, seq, width), BF16),
            jax.ShapeDtypeStruct((n, pad, width), F32),
            jax.ShapeDtypeStruct((n, pad, width), BF16),
            jax.ShapeDtypeStruct((8, width), F32),
        ],
        grid_spec=grid_spec,
        compiler_params=params(60),
        cost_estimate=pl.CostEstimate(
            flops=12 * rows * width * hidden, bytes_accessed=40 * MIB, transcendentals=rows * hidden),
        name="feed",
    )(counts, depth, a2, gm, up, down, bu.reshape(steps, 1, block), x1, cot, bd, gain)


def back_kernel(pad, counts, ga_ref, w_ref, qkv_ref, lse_ref, g_ref, go):
    i = pl.program_id(0)
    width = ga_ref.shape[-1]
    count = counts[i]
    go[...] = nt(ga_ref[0], w_ref[...]).astype(BF16)
    ok = lax.broadcasted_iota(jnp.int32, (pad, pad), 0) < count
    lane = lax.broadcasted_iota(jnp.int32, (pad, 128), 1)

    def pair(p):
        at = pl.multiple_of(p * 128, 128)
        q = qkv_ref[0, :, pl.ds(at, 128)] * 0.125
        k = qkv_ref[0, :, pl.ds(width + at, 128)]
        v = qkv_ref[0, :, pl.ds(2 * width + at, 128)]
        g = go[:, pl.ds(at, 128)]
        gq = jnp.zeros((pad, 128), F32)
        gk = jnp.zeros((pad, 128), F32)
        gv = jnp.zeros((pad, 128), F32)
        for half in range(2):
            mine = (lane >= 64) if half else (lane < 64)
            qm = jnp.where(mine, q, 0)
            km = jnp.where(mine, k, 0) * 0.125
            gmine = jnp.where(mine, g, 0)
            scores = nt(k, qm)
            row = lse_ref[0, 2 * p + half:2 * p + half + 1, :]
            prob = jnp.where(ok, jnp.exp(scores - row), 0.0)
            dp = nt(v, gmine)
            inner = col_sum(prob * dp)
            ds = (prob * (dp - inner)).astype(BF16)
            gv = gv + nn(prob.astype(BF16), gmine)
            gk = gk + nn(ds, qm)
            gq = gq + tn(ds, km)
        g_ref[0, :, pl.ds(at, 128)] = gq.astype(BF16)
        g_ref[0, :, pl.ds(width + at, 128)] = gk.astype(BF16)
        g_ref[0, :, pl.ds(2 * width + at, 128)] = gv.astype(BF16)

    for p in range(width // 128):
        pair(p)


def back(counts, ga, w, qkv, lse):
    n, pad, width = ga.shape
    grid_spec = pltpu.PrefetchScalarGridSpec(
        num_scalar_prefetch=1,
        grid=(n,),
        in_specs=[by_image((pad, width)), whole(w.shape), by_image((pad, 3 * width)), by_image((16, pad))],
        out_specs=[by_image((pad, 3 * width))],
        scratch_shapes=[pltpu.VMEM((pad, width), BF16)],
    )
    return pl.pallas_call(
        functools.partial(back_kernel, pad),
        out_shape=[jax.ShapeDtypeStruct((n, pad, 3 * width), BF16)],
        grid_spec=grid_spec,
        compiler_params=params(40),
        cost_estimate=pl.CostEstimate(
            flops=2 * n * pad * width * (width + 10 * pad), bytes_accessed=16 * MIB,
            transcendentals=n * 12 * pad * pad),
        name="back",
    )(counts, ga, w, qkv, lse)[0]


def outgrad_kernel(o_ref, ga_ref, d_ref):
    d_ref[...] = tn(o_ref[...], ga_ref[...]).astype(BF16)


def outgrad(o, ga):
    rows, width = o.shape
    return pl.pallas_call(
        outgrad_kernel,
        out_shape=jax.ShapeDtypeStruct((width, width), BF16),
        grid=(2,),
        in_specs=[pl.BlockSpec((rows, width // 2), lambda j: (0, j)), whole(ga.shape)],
        out_specs=pl.BlockSpec((width // 2, width), lambda j: (j, 0)),
        compiler_params=params(32),
        cost_estimate=pl.CostEstimate(
            flops=2 * rows * width * width, bytes_accessed=6 * MIB, transcendentals=0),
        name="outgrad",
    )(o, ga)


def last_kernel(seq, pad, g_ref, a1_ref, w_ref, x_ref, gx_ref, gain_ref,
                d_ref, cols_ref, gi_ref, vec_ref, ga1, xs):
    c = pl.program_id(0)
    n = x_ref.shape[0]
    g = g_ref[...]
    d_ref[...] = tn(g, a1_ref[...]).astype(BF16)
    cols_ref[...] = col_sum(g.astype(F32))
    part = nn(g, w_ref[...])

    @pl.when(c == 0)
    def _():
        ga1[...] = part

    @pl.when(c > 0)
    def _():
        ga1[...] += part

    @pl.when(c == pl.num_programs(0) - 1)
    def _():
        width = x_ref.shape[-1]
        xs[pad - 8:pad, :] = jnp.zeros((8, width), F32)
        ggain = jnp.zeros((1, width), F32)
        gshift = jnp.zeros((1, width), F32)
        for i in range(n):
            xs[0:seq, :] = x_ref[i].astype(F32)
            normed, rstd = normalize(xs[...])
            grad = ga1[i * pad:(i + 1) * pad, :]
            ggain = ggain + col_sum(grad * normed)
            gshift = gshift + col_sum(grad)
            e = grad * gain_ref[...]
            gi = gx_ref[i] + rstd * (e - mean_row(e) - normed * mean_row(e * normed))
            gi_ref[i] = gi[0:seq]
        vec_ref[0:1, :] = ggain
        vec_ref[1:2, :] = gshift
        vec_ref[2:8, :] = jnp.zeros((6, width), F32)


def last(g, a1, w, images, gx, gain, pad, block=384):
    n, seq, width = images.shape
    rows, total = g.shape
    return pl.pallas_call(
        functools.partial(last_kernel, seq, pad),
        out_shape=[
            jax.ShapeDtypeStruct((total, width), BF16),
            jax.ShapeDtypeStruct((1, total), F32),
            jax.ShapeDtypeStruct((n, seq, width), F32),
            jax.ShapeDtypeStruct((8, width), F32),
        ],
        grid=(total // block,),
        in_specs=[
            pl.BlockSpec((rows, block), lambda c: (0, c)), whole(a1.shape),
            pl.BlockSpec((block, width), lambda c: (c, 0)), whole(images.shape), whole(gx.shape),
            whole(gain.shape),
        ],
        out_specs=[
            pl.BlockSpec((block, width), lambda c: (c, 0)), pl.BlockSpec((1, block), lambda c: (0, c)),
            whole((n, seq, width)), whole((8, width)),
        ],
        scratch_shapes=[pltpu.VMEM((rows, width), F32), pltpu.VMEM((pad, width), F32)],
        compiler_params=params(50),
        cost_estimate=pl.CostEstimate(
            flops=4 * rows * width * total, bytes_accessed=30 * MIB, transcendentals=0),
        name="last",
    )(g, a1, w, images, gx, gain)


def shards(
    images, grid_sizes, keep_flags, attn_gain, attn_shift, attend_weight, query_bias, value_bias,
    output_weight, output_bias, mlp_gain, mlp_shift, up_weight, up_bias, down_weight, down_bias,
    cotangent,
):
    n, seq, width = images.shape
    pad = -(-seq // 32) * 32
    counts = grid_sizes[:, 0] * grid_sizes[:, 1] + 2
    depth = keep_flags.astype(F32) / KEEP_PROB
    owners = width // attn_gain.shape[0]

    small = jnp.concatenate([
        attn_gain, attn_shift, query_bias, value_bias, output_bias, mlp_gain, mlp_shift, down_bias, up_bias])
    small = lax.all_gather(small.reshape(1, -1), "fsdp", axis=0, tiled=True).astype(F32)
    share = attn_gain.shape[0]
    vec = [small[:, k * share:(k + 1) * share].reshape(1, width) for k in range(8)]
    bu = small[:, 8 * share:].reshape(1, -1)
    gain_one, shift_one, bias_q, bias_v, bias_o, gain_two, shift_two, bias_d = vec
    bias = jnp.concatenate([bias_q, jnp.zeros_like(bias_q), bias_v], 1)

    attend = lax.all_gather(attend_weight.T, "fsdp", axis=0, tiled=True)
    out_w = lax.all_gather(output_weight, "fsdp", axis=0, tiled=True)
    up = lax.all_gather(up_weight.T, "fsdp", axis=0, tiled=True)
    down = lax.all_gather(down_weight, "fsdp", axis=0, tiled=True)

    a1, gm, qkv, o, lse = front(counts, depth, images, cotangent, attend, gain_one, shift_one, bias, pad)
    x1, a2, sums_two = middle(counts, depth, o, images, out_w, bias_o, gain_two, shift_two, pad)
    flat = lambda array: array.reshape(n * pad, array.shape[-1])
    block = up_weight.shape[1] if up_weight.shape[1] % 128 == 0 else 384
    dup, ddown, gbu, y, gx, ga, vec_feed = feed(
        counts, depth, flat(a2), flat(gm), up, down, bu, x1, cotangent, bias_d, gain_two, seq, pad, block)
    dout = outgrad(flat(o), flat(ga))
    g = back(counts, ga, out_w, qkv, lse)
    dattend, cols, gi, vec_last = last(flat(g), flat(a1), attend, images, gx, gain_one, pad)

    sums = jnp.stack([jnp.sum(sums_two[:, 0]), jnp.sum(sums_two[:, 1]), jnp.sum(vec_feed[4]),
                      jnp.sum(counts).astype(F32)])

    def spread(array):
        return lax.psum(lax.psum_scatter(array, "fsdp", scatter_dimension=0, tiled=True), "dp")

    def columns(array):
        hidden = up.shape[0]
        array = jnp.swapaxes(array, 0, 1).reshape(width, owners, hidden // owners)
        return jnp.swapaxes(array, 0, 1)

    gup = spread(columns(dup))[0]
    gdown = spread(columns(ddown))[0].T
    gout = spread(dout)
    gattend = spread(dattend).T
    rows = jnp.concatenate([
        vec_last[0:2], cols[:, :width], cols[:, 2 * width:], vec_feed[3:4], vec_feed[0:3],
    ], 0)
    tiny = jnp.concatenate([
        jnp.swapaxes(rows.reshape(8, owners, share), 0, 1).reshape(owners, 8 * share),
        gbu.reshape(owners, -1)], 1)
    tiny = spread(tiny)[0]
    sums = lax.psum(sums, ("dp", "fsdp"))
    root_means = jnp.sqrt(sums[:3] / (sums[3] * width))
    tv = [tiny[k * share:(k + 1) * share] for k in range(8)]
    f = lambda array: array.astype(F32)
    return (y, gi, tv[0], tv[1], f(gattend), tv[2], tv[3], f(gout), tv[4], tv[5], tv[6],
            f(gup), tiny[8 * share:], f(gdown), tv[7], root_means)


def solution(mesh):
    images = P(("dp", "fsdp"), None, None)
    flags = P(("dp", "fsdp"), None)
    vec, rows, cols = P("fsdp"), P("fsdp", None), P(None, "fsdp")
    return jax.shard_map(
        shards,
        mesh=mesh,
        in_specs=(images, flags, flags, vec, vec, cols, vec, vec, rows, vec, vec, vec, cols, vec, rows,
                  vec, images),
        out_specs=(images, images, vec, vec, cols, vec, vec, rows, vec, vec, vec, cols, vec, rows, vec,
                   P()),
        check_vma=False,
    )
```

time: 705 us -> 561 us (0.80)
  matrix products: 173 us -> 0 us
  Pallas kernels: 0 us -> 136 us
  other arithmetic: 81 us -> 11.6 us
  blocking collectives: 120 us -> 91.1 us
  local copies, waits for them, and re-layouts: 65.5 us -> 53.5 us
  waiting for transfers between devices: 242 us -> 252 us
    dot_general x26 -> x0, matrix products: 173 us -> none  [product(): return jnp.einsum(formula, left, right, preferred_element_type=jnp.float32)]
    pallas_call x0 -> x6, Pallas kernels: none -> 136 us  [the longest x1 65.6 us: feed(): pl.pallas_call(functools.partial(feed_kernel, seq, pad), out_shape=[jax.S...]
    all_gather x4, waiting for transfers between devices: 6.62 us -> 96.2 us  [the longest x1 52 us: shards(): down = lax.all_gather(down_weight, 'fsdp', axis=0, tiled=True)]
    reduce_scatter x4, waiting for transfers between devices: 233 us -> 153 us  [spread(): lax.psum_scatter(array, 'fsdp', scatter_dimension=0, tiled=True)]
    convert_element_type x30 -> x4, other arithmetic: 60.6 us -> 3.95 us  [the longest x3 3.94 us: shards(): f = lambda array: array.astype(F32)]
    unnamed x2 -> x1, blocking collectives: 58.9 us -> 27.1 us
    unnamed x134 -> x101, local copies, waits for them, and re-layouts: 23.5 us -> 42.7 us
    convert_element_type x2 -> x0, local copies, waits for them, and re-layouts: 12.4 us -> none  [the longest x1 8.38 us: shards(): (product('bld,de->ble', ln_first, attend_whole) + bias_joint).astype(jnp....]
  transfers between devices with their start and end apart: 9 -> 9, of which waited for: 4 -> 6; matrix products, arithmetic and copies ran while one was open for 35% -> 6% of each run, Pallas kernels for 0% -> 12%
where the time goes in v1:
time: 561 us; the launch traced here: 560 us
  waiting for transfers between devices  252 us (45%)
  Pallas kernels  136 us (24%)
  blocking collectives  91.1 us (16%)
  local copies, waits for them, and re-layouts  53.5 us (10%)
  between operations  15.6 us (3%)
  other arithmetic  11.6 us (2%)
    reduce_scatter x4, waiting for transfers between devices, spread(): lax.psum_scatter(array, 'fsdp', scatter_dimension=0, tiled=True)  153 us
    pallas_call x1, Pallas kernels, feed(): pl.pallas_call(functools.partial(feed_kernel, seq, pad), out_shape=[jax.S...  65.6 us
    all_gather x1, waiting for transfers between devices, shards(): down = lax.all_gather(down_weight, 'fsdp', axis=0, tiled=True)  52 us
    unnamed x101, local copies, waits for them, and re-layouts  42.7 us
    psum x1, blocking collectives, shards(): sums = lax.psum(sums, ('dp', 'fsdp'))  38.4 us
    all_gather x1, waiting for transfers between devices, shards(): up = lax.all_gather(up_weight.T, 'fsdp', axis=0, tiled=True)  32.9 us
    unnamed x1, blocking collectives  27.1 us
    pallas_call x1, Pallas kernels, front(): pl.pallas_call(functools.partial(front_kernel, seq, pad), out_shape=[jax....  22.3 us
  transfers between devices with their start and end apart: 9, of which 6 were waited for; matrix products, arithmetic and copies ran while one was open for 6% of the time, Pallas kernels for 12%

profile of v1, /device:TPU:0, one launch (start us, length us, event | category | flops | bytes accessed | tf_op | source)
XLA Modules:
  0.0 560.1 jit_solution(7740042532064597481)
XLA Ops:
  8.1 0.7 all-gather.9.cloned.1.call-update
  8.8 2.1 copy.49
  11.8 15.8 %all-gather.1 = bf16[8,1,1152]{2,1,0:T(2,128)(2,1)S(1)} all-gather(bf16[1,1,1152]{2,1,0:T(2,128)(2,1)S(1)} %reshape.124), channel_id=2, replica_groups=mesh['dp'=4,'fsdp'=8] {'fsdp'}, dimensions={0}, use_global_device_ids=true | all-gather | bytes 20736 | tf_op jit(solution)/shard_map/all_gather | solution.py:471
  31.2 1.7 copy.47.cot_ref
  32.9 1.4 reshape.110.gain_ref
  34.3 1.3 reshape.109.bias_ref
  35.6 1.3 reshape.111.shift_ref
  37.0 1.4 reshape.114.bd_ref
  39.0 1.9 fusion.1
  40.9 1.3 convert_multiply_fusion.depth
  42.1 0.7 fusion.bias_ref
  42.8 11.3 %all-gather.7.cloned.1.call-done.w_ref = bf16[2304,768]{1,0:T(8,128)(2,1)} async-done(((bf16[288,768]{1,0:T(8,128)(2,1)}), bf16[2304,768]{1,0:T(8,128)(2,1)}) %all-gather.7.cloned.1.call-update) | async-done | bytes 3538960 | tf_op jit(solution)/shard_map/all_gather | solution.py:478
  56.1 2.0 copy-done.10
  58.1 22.3 %front.1 = (bf16[4,288,768]{2,1,0:T(8,128)(2,1)S(1)}, bf16[4,288,768]{2,1,0:T(8,128)(2,1)S(1)}, bf16[4,288,2304]{2,1,0:T(8,128)(2,1)}, bf16[4,288,768]{2,1,0:T(8,128)(2,1)S(1)}, f32[4,16,288]{2,1,0:T(8,128)S(1)}) custom-call(s32[4]{0:T(128)S(1)} %bitcast.44, f32[4,2]{1,0:T(4,128)S(1)} %copy-done.5, bf16[4,282,768]{2,1,0:T(8,128)(2,1)S(1)} %copy.46.x_ref, ...), custom_call_target="tpu_custom_call" | custom-call | flops 6115295232 | bytes 20971520 | tf_op jit(solution)/shard_map/front/pallas_call | solution.py:123
  80.5 1.2 copy-done.14
  81.7 1.2 copy-done.16
  82.9 1.2 copy-done.19
  88.1 1.3 copy-done.11
  89.4 1.5 copy-done.17
  90.9 4.2 middle.1
  95.1 1.3 copy-done.22
  96.4 1.8 copy-done.23
  98.1 32.9 %all-gather.11.cloned.1.call-done.up_ref = bf16[3072,768]{1,0:T(8,128)(2,1)} async-done(((bf16[384,768]{1,0:T(8,128)(2,1)}), bf16[3072,768]{1,0:T(8,128)(2,1)}) %all-gather.11.cloned.1.call-update) | async-done | bytes 4718608 | tf_op jit(solution)/shard_map/all_gather | solution.py:480
  131.0 52.0 %all-gather.13.cloned.1.call-done.down_ref = bf16[3072,768]{1,0:T(8,128)(2,1)} async-done(((bf16[384,768]{1,0:T(8,128)(2,1)}), bf16[3072,768]{1,0:T(8,128)(2,1)}) %all-gather.13.cloned.1.call-update) | async-done | bytes 4718608 | tf_op jit(solution)/shard_map/all_gather | solution.py:481
  183.1 65.6 %feed.1 = (bf16[8,768,384]{2,1,0:T(8,128)(2,1)}, bf16[8,768,384]{2,1,0:T(8,128)(2,1)}, f32[8,1,384]{2,1,0:T(1,128)}, bf16[4,282,768]{2,1,0:T(8,128)(2,1)}, f32[4...) custom-call(s32[4]{0:T(128)} %bitcast.43, f32[4,2]{1,0:T(4,128)} %convert_multiply_fusion.depth, ...), custom_call_target="tpu_custom_call" | custom-call | flops 32614907904 | bytes 41943040 | tf_op jit(solution)/shard_map/feed/pallas_call | solution.py:294
  248.6 1.5 copy-done.18
  250.1 1.5 copy-done.20
  251.6 3.0 outgrad.1
  254.7 1.5 copy-done.21
  256.2 2.5 copy-done.24
  258.7 19.8 %back.1 = bf16[4,288,2304]{2,1,0:T(8,128)(2,1)S(1)} custom-call(s32[4]{0:T(128)S(1)} %bitcast.46, bf16[4,288,768]{2,1,0:T(8,128)(2,1)S(1)} %copy-done.21, bf16[768,768]{1,0:T(8,128)(2,1)S(1)} %copy-done.12, bf16[4,288,2304]{2,1,0:T(8,128)(2,1)S(1)} %copy-done.24, f32[4,16,288]{2,1,0:T(8,128)S(1)} %copy-done.26), custom_call_target="tpu_custom_call" | custom-call | flops 6455033856 | bytes 16777216 | tf_op jit(solution)/shard_map/back/pallas_call | solution.py:361
  278.5 2.4 copy-done.13
  280.8 20.7 %last.1 = (bf16[2304,768]{1,0:T(8,128)(2,1)}, f32[1,2304]{1,0:T(1,128)S(1)}, f32[4,282,768]{2,1,0:T(8,128)}, f32[8,768]{1,0:T(8,128)S(1)}) custom-call(bf16[1152,2304]{1,0:T(8,128)(2,1)} %bitcast.47, bf16[1152,768]{1,0:T(8,128)(2,1)S(1)} %bitcast.48, bf16[2304,768]{1,0:T(8,128)(2,1)} %all-gather.7.cloned.1.call-done.w_ref, ...), custom_call_target="tpu_custom_call" | custom-call | flops 8153726976 | bytes 31457280 | tf_op jit(solution)/shard_map/last/pallas_call | solution.py:432
  301.6 0.7 reduce-scatter.9.cloned.1.call-update
  302.3 0.7 reduce-scatter.11.cloned.1.call-update
  303.2 41.2 %reduce-scatter.5.cloned.1.call-done = bf16[288,768]{1,0:T(8,128)(2,1)} async-done(((bf16[2304,768]{1,0:T(8,128)(2,1)}), bf16[288,768]{1,0:T(8,128)(2,1)}) %reduce-scatter.5.cloned.1.call-update) | async-done | bytes 442384 | tf_op jit(solution)/shard_map/reduce_scatter | solution.py:497
  344.3 55.9 %reduce-scatter.9.cloned.1.call-done = bf16[1,768,384]{2,1,0:T(8,128)(2,1)} async-done(((bf16[8,768,384]{2,1,0:T(8,128)(2,1)}), bf16[1,768,384]{2,1,0:T(8,128)(2,1)}) %reduce-scatter.9.cloned.1.call-update) | async-done | bytes 589840 | tf_op jit(solution)/shard_map/reduce_scatter | solution.py:497
  400.2 55.7 %reduce-scatter.11.cloned.1.call-done = bf16[1,768,384]{2,1,0:T(8,128)(2,1)} async-done(((bf16[8,768,384]{2,1,0:T(8,128)(2,1)}), bf16[1,768,384]{2,1,0:T(8,128)(2,1)}) %reduce-scatter.11.cloned.1.call-update) | async-done | bytes 589840 | tf_op jit(solution)/shard_map/reduce_scatter | solution.py:497
  457.9 2.0 pad_maximum_fusion.1
  460.5 38.4 %psum.47 = f32[4]{0:T(128)S(1)} all-reduce(f32[4]{0:T(128)S(1)} %pad_maximum_fusion.1), channel_id=1, replica_groups=mesh['dp'=4,'fsdp'=8] {'dp','fsdp'}, use_global_device_ids=true, to_apply=%region_14.0 | all-reduce | flops 4 | bytes 32 | tf_op jit(solution)/shard_map/psum | solution.py:515
  499.7 6.1 %copy.54 = f32[4,282,768]{2,0,1:T(4,128)} copy(f32[4,282,768]{2,1,0:T(8,128)} %get-tuple-element.71) | data formatting | bytes 6930432
  505.8 2.5 copy.53
  509.0 27.1 %all-reduce = f32[8,1152]{1,0:T(8,128)S(1)} all-reduce(f32[8,1152]{1,0:T(8,128)S(1)} %pad_maximum_fusion), channel_id=3, replica_groups=mesh['dp'=4,'fsdp'=8] {'fsdp'}, use_global_device_ids=true, to_apply=%region_0.0.clone | all-reduce | flops 9216 | bytes 73728
  536.8 9.9 %psum.42 = f32[1,1152]{1,0:T(1,128)S(1)} all-reduce(f32[1,1152]{1,0:T(1,128)S(1)} %constant_dynamic-slice_fusion), channel_id=1, replica_groups=mesh['dp'=4,'fsdp'=8] {'dp'}, use_global_device_ids=true, to_apply=%region_1.0 | all-reduce | flops 1152 | bytes 9216 | tf_op jit(solution)/shard_map/psum | solution.py:497
  548.4 2.2 convert_element_type.39
  550.6 1.3 copy.55
  551.9 1.0 convert_element_type.36
  552.9 0.7 convert_element_type.37
  (126 shorter events, 17.2 us)
Async XLA Ops:
  7.2 4.4 copy-start.36
  7.2 4.4 copy-start.37
  7.2 4.4 copy-start.38
  7.2 4.4 copy-start.39
  7.2 4.4 copy-start.40
  7.2 4.4 copy-start.41
  7.2 4.4 copy-start.42
  7.3 4.4 copy-start.34
  7.3 4.4 copy-start.43
  7.3 23.0 %copy-start.28 = (bf16[4,282,768]{2,0,1:T(4,128)(2,1)S(1)}, bf16[4,282,768]{2,0,1:T(4,128)(2,1)}, u32[]{:S(2)}) copy-start(bf16[4,282,768]{2,0,1:T(4,128)(2,1)} %param.17) | copy-start | bytes 5197828
  7.3 46.8 %all-gather.7.cloned.1.call-start = ((), (), s32[]{:S(2)}) async-start(), calls=%async_computation.4 | async-start | bytes 3981312 | tf_op jit(solution)/shard_map/all_gather | solution.py:478
  8.0 76.7 %all-gather.9.cloned.1.call-start = ((), (), s32[]{:S(2)}) async-start(), calls=%async_computation.5 | async-start | bytes 1327104 | tf_op jit(solution)/shard_map/all_gather | solution.py:479
  8.8 122.2 %all-gather.11.cloned.1.call-start = ((), (), s32[]{:S(2)}) async-start(), calls=%async_computation.6 | async-start | bytes 5308416 | tf_op jit(solution)/shard_map/all_gather | solution.py:480
  11.0 172.1 %all-gather.13.cloned.1.call-start = ((), (), s32[]{:S(2)}) async-start(), calls=%async_computation.7 | async-start | bytes 5308416 | tf_op jit(solution)/shard_map/all_gather | solution.py:481
  11.5 291.6 %reduce-scatter.7.cloned.1.call-start = ((), (), s32[]{:S(2)}) async-start(), calls=%async_computation.9 | async-start | bytes 1327104 | tf_op jit(solution)/shard_map/reduce_scatter | solution.py:497
  28.3 2.3 copy-start.35
  32.9 47.6 %copy-start = (bf16[4,282,768]{2,1,0:T(8,128)(2,1)}, bf16[4,282,768]{2,1,0:T(8,128)(2,1)S(1)}, u32[]{:S(2)}) copy-start(bf16[4,282,768]{2,1,0:T(8,128)(2,1)S(1)} %copy.47.cot_ref) | copy-start | bytes 5197828
  54.1 0.7 copy-start.4
  56.1 2.0 copy-start.10
  80.5 1.2 copy-start.14
  81.7 1.2 copy-start.16
  82.9 1.2 copy-start.19
  85.4 0.7 copy-start.2
  86.1 0.7 copy-start.3
  88.1 1.3 copy-start.11
  89.4 1.5 copy-start.17
  95.1 1.3 copy-start.22
  96.4 1.8 copy-start.23
  248.6 1.5 copy-start.18
  250.1 1.5 copy-start.20
  251.6 3.1 copy-start.9
  251.6 3.1 copy-start.12
  251.6 3.1 copy-start.26
  254.6 89.7 %reduce-scatter.5.cloned.1.call-start = ((), (), s32[]{:S(2)}) async-start(), calls=%async_computation.8 | async-start | bytes 3981312 | tf_op jit(solution)/shard_map/reduce_scatter | solution.py:497
  254.7 1.5 copy-start.21
  256.2 2.5 copy-start.24
  258.7 22.2 %copy-start.15 = (bf16[4,288,768]{2,1,0:T(8,128)(2,1)S(1)}, bf16[4,288,768]{2,1,0:T(8,128)(2,1)}, u32[]{:S(2)}) copy-start(bf16[4,288,768]{2,1,0:T(8,128)(2,1)} %copy-done.14) | copy-start | bytes 5308420
  278.5 2.4 copy-start.13
  301.5 98.7 %reduce-scatter.9.cloned.1.call-start = ((), (), s32[]{:S(2)}) async-start(), calls=%async_computation.10 | async-start | bytes 5308416 | tf_op jit(solution)/shard_map/reduce_scatter | solution.py:497
  302.3 153.7 %reduce-scatter.11.cloned.1.call-start = ((), (), s32[]{:S(2)}) async-start(), calls=%async_computation.11 | async-start | bytes 5308416 | tf_op jit(solution)/shard_map/reduce_scatter | solution.py:497
  303.0 154.2 %copy-start.32 = (f32[8,768]{1,0:T(8,128)S(1)}, f32[8,768]{1,0:T(8,128)}, u32[]{:S(2)}) copy-start(f32[8,768]{1,0:T(8,128)} %get-tuple-element.48) | copy-start | bytes 73732
  303.1 156.8 %copy-start.44 = (u32[32]{0:T(128)S(1)}, u32[32]{0:T(128)}, u32[]{:S(2)}) copy-start(u32[32]{0:T(128)} %constant.19) | copy-start | bytes 388
  303.1 196.6 %copy-start.33 = (f32[8,1,384]{2,1,0:T(1,128)S(1)}, f32[8,1,384]{2,1,0:T(1,128)}, u32[]{:S(2)}) copy-start(f32[8,1,384]{2,1,0:T(1,128)} %get-tuple-element.49) | copy-start | bytes 36868
  303.1 245.3 %all-reduce.4.cloned.1.call-start = ((), (), s32[]{:S(2)}) async-start(), calls=%async_computation.12 | async-start | bytes 3538944 | tf_op jit(solution)/shard_map/psum | solution.py:497
  499.7 6.1 %copy-start.27 = (bf16[4,282,768]{2,1,0:T(8,128)(2,1)S(1)}, bf16[4,282,768]{2,1,0:T(8,128)(2,1)}, u32[]{:S(2)}) copy-start(bf16[4,282,768]{2,1,0:T(8,128)(2,1)} %get-tuple-element.70) | copy-start | bytes 5197828
  548.3 2.3 copy-start.29
  548.3 3.5 copy-start.30
  550.6 2.3 copy-start.31
  (6 other events, 4.0 us)
Sparse Core Ops, SparseCore 0:
  9.8 44.3 all-gather.6
  55.8 21.4 all-gather.8
  79.5 51.4 all-gather.10
  132.5 50.5 all-gather.12
  254.7 31.4 reduce-scatter.6
  301.7 42.6 reduce-scatter.4
  346.7 53.4 reduce-scatter.8
  402.6 53.2 reduce-scatter.10
  459.8 63.5 all-reduce.3
